TPU v7x, 32 devices: a whole 2x2x4 slice. The times are simulated.
32 devices in a mesh: tm: 4 (over y, x), pts: 8 (over z, core).
Axes of the slice: x: 2, y: 2, z: 4, core: 2. Of those that a mesh axis runs over, the one named last changes fastest.
Arguments:
- series: bfloat16 [8192, 3, 8192], P('tm', None, 'pts'), may hold values from -6 to 6
- weights: float32 [8192], P('pts'), may hold values from 1.2207031e-05 to 0.00012207031
- freq_bins: int32 [16], replicated, may hold values from 1 to 255
Outputs:
- cross_gram: float32 [16, 2, 32, 32], P('tm')
- spatial_modes: bfloat16 [16, 2, 32, 3, 8192], P('tm', None, None, None, 'pts')
All inputs are finite; a program needn't handle non-finite values.
Results may differ from a plain program's by a relative error of at most 0.0067.
Values may be sent and summed in bfloat16 or wider, within the bound.
A program may use at most 128 MiB of HBM per device.

v0:
```python
import functools

import jax
import jax.numpy as jnp
from jax import lax
from jax.experimental import pallas as pl
from jax.experimental.pallas import tpu as pltpu
from jax.sharding import PartitionSpec as P

NFFT = 512
NB = 32
NF = 16
ITERS = 4
HALF = NFFT // 2
CHUNK = 256
MESH = pl.DeviceIdType.MESH
F32 = jnp.float32
BF16 = jnp.bfloat16


def build_table(freq_bins):
    sample_index = jnp.arange(NFFT, dtype=jnp.int32)
    window = (
        0.5 - 0.5 * jnp.cos(2.0 * jnp.pi * sample_index.astype(jnp.float32) / NFFT)
    ) * jnp.sqrt(8.0 / (3.0 * NFFT))
    product_index = freq_bins[:, None] * sample_index[None, :] % NFFT
    phase_angle = 2.0 * jnp.pi * product_index.astype(jnp.float32) / NFFT
    kernel_table = jnp.stack(
        [jnp.cos(phase_angle) * window, -jnp.sin(phase_angle) * window], axis=1
    )
    return kernel_table.reshape(2 * NF, NFFT).astype(jnp.bfloat16)


def dot_high(left, right):
    return jnp.dot(
        left, right, precision=lax.Precision.HIGHEST, preferred_element_type=F32
    )


def dot_t(left, right, **kw):
    return lax.dot_general(
        left, right, (((1,), (1,)), ((), ())), preferred_element_type=F32, **kw
    )


def eye(size):
    row = lax.broadcasted_iota(jnp.int32, (size, size), 0)
    col = lax.broadcasted_iota(jnp.int32, (size, size), 1)
    return (row == col).astype(F32)


def gather_order(rows, lb, lf):
    new = lax.broadcasted_iota(jnp.int32, (rows, rows), 0)
    old = lax.broadcasted_iota(jnp.int32, (rows, rows), 1)
    per = 2 * lf
    old_new = (old % per) * NB + old // per
    return (new == old_new).astype(F32)


def normalized(real, imag):
    norm = jnp.sqrt(
        jnp.sum(real * real + imag * imag, axis=(0, 1), keepdims=True)
    )
    upper = jnp.concatenate([real, -imag], axis=1)
    lower = jnp.concatenate([imag, real], axis=1)
    return jnp.concatenate([upper, lower], axis=0) / norm


def inverse_roots(ys):
    ident = eye(2 * NB)
    zs = None
    for it in range(ITERS):
        zys = ys if zs is None else [dot_high(z, y) for z, y in zip(zs, ys)]
        steps = [0.5 * (3.0 * ident - zy) for zy in zys]
        if it < ITERS - 1:
            ys = [dot_high(y, s) for y, s in zip(ys, steps)]
        zs = steps if zs is None else [dot_high(s, z) for s, z in zip(steps, zs)]
    return zs


def kernel(nt, ns, series, table_ref, w_ref, total_ref, rows_ref,
           xbuf, send, land, xall, pair, ring, in_sem, a2a_send, a2a_recv,
           core_send, core_recv, ar_send, ar_recv, row_sem):
    t = lax.axis_index("tm")
    s = lax.axis_index("pts")
    points = xbuf.shape[2]
    cuts = [0, *range(CHUNK // 2, points, CHUNK), points]
    nq = len(cuts) - 1

    def span(q):
        return pl.ds(cuts[q], cuts[q + 1] - cuts[q])

    lb = NB // nt
    lf = NF // nt
    per = 2 * lf
    part = lb * per
    rows = nt * part
    for q in range(nq):
        pltpu.make_async_copy(
            series.at[:, :, span(q)], xbuf.at[:, :, span(q)], in_sem.at[q]
        ).start()
    barrier = pltpu.get_barrier_semaphore()
    for k in range(1, nt):
        pl.semaphore_signal(barrier, inc=1, device_id={"tm": lax.rem(t + k, nt)},
                            device_id_type=MESH)
    other = s + 1 - 2 * lax.rem(s, 2)
    nz = ns // 2
    pl.semaphore_signal(barrier, inc=1, device_id={"pts": other}, device_id_type=MESH)
    for k in range(1, nz):
        pl.semaphore_signal(barrier, inc=1,
                            device_id={"pts": lax.rem(s + 2 * k, ns)},
                            device_id_type=MESH)
    pl.semaphore_wait(barrier, nt - 1 + nz)

    def peer_copy(q, k):
        to = lax.rem(t + k, nt)
        return pltpu.make_async_remote_copy(
            src_ref=send.at[to, :, span(q)], dst_ref=land.at[k, :, span(q)],
            send_sem=a2a_send.at[q, k], recv_sem=a2a_recv.at[q, k],
            device_id={"tm": to}, device_id_type=MESH,
        )

    order = gather_order(rows, lb, lf).astype(BF16)
    gram = jnp.zeros((rows, rows), F32)

    def row_copy(q):
        cols = span(q)
        return pltpu.make_async_copy(
            xall.at[:, :, cols], rows_ref.at[:, :, cols], row_sem.at[q]
        )

    def consume(q, gram):
        cols = span(q)
        for k in range(1, nt):
            peer_copy(q, k).wait_recv()
        weight = w_ref[:, cols]
        halos = [
            land[lax.rem(t - src - 1 + nt, nt), 3 * part:, cols].astype(F32)
            for src in range(nt)
        ]
        for c in range(3):
            for src in range(nt):
                at = lax.rem(t - src + nt, nt)
                main = part - 2 * per
                xall[c, src * part:src * part + main, cols] = land[at, c * part:c * part + main, cols]
                tail = land[at, c * part + main:(c + 1) * part, cols].astype(F32)
                fixed = tail[per:] + halos[src][c * per:(c + 1) * per]
                xall[c, src * part + main:(src + 1) * part, cols] = jnp.concatenate(
                    [tail[:per], fixed], axis=0).astype(BF16)
            x = jnp.dot(
                order, xall[c, :, cols], preferred_element_type=F32
            ).astype(BF16)
            xall[c, :, cols] = x
            xw = x.astype(F32) * weight
            hi = xw.astype(BF16)
            lo = (xw - hi.astype(F32)).astype(BF16)
            gram = gram + dot_t(hi, x) + dot_t(lo, x)
        row_copy(q).start()
        return gram

    for q in range(nq):
        pltpu.make_async_copy(
            series.at[:, :, span(q)], xbuf.at[:, :, span(q)], in_sem.at[q]
        ).wait()
        edges = []
        for c in range(3):
            firsts, seconds = [], []
            for j in range(lb):
                block = xbuf[c, j * HALF:(j + 1) * HALF, span(q)]
                both = jnp.dot(table_ref[...], block, preferred_element_type=F32)
                firsts.append(both[:2 * NF])
                seconds.append(both[2 * NF:])
            sums = [firsts[j] + seconds[j + 1] for j in range(lb - 1)]
            sums.append(firsts[lb - 1])
            edges.append(seconds[0])
            for d in range(nt):
                send[d, c * part:(c + 1) * part, span(q)] = jnp.concatenate(
                    [v[d * per:(d + 1) * per] for v in sums], axis=0
                ).astype(BF16)
        edges.append(jnp.zeros(edges[0].shape, F32))
        for d in range(nt):
            send[d, 3 * part:, span(q)] = jnp.concatenate(
                [v[d * per:(d + 1) * per] for v in edges], axis=0
            ).astype(BF16)
        for k in range(1, nt):
            peer_copy(q, k).start()
        land[0, :, span(q)] = send[t, :, span(q)]
        if q > 0:
            gram = consume(q - 1, gram)
    gram = consume(nq - 1, gram)

    parts = []
    for f in range(lf):
        a = f * 2 * NB
        b = a + NB
        e = b + NB
        parts.append(gram[a:b, a:b] + gram[b:e, b:e])
        parts.append(gram[a:b, b:e] - gram[b:e, a:b])
    pair[0] = jnp.concatenate(parts, axis=1)

    core_copy = pltpu.make_async_remote_copy(
        src_ref=pair.at[0], dst_ref=pair.at[1], send_sem=core_send,
        recv_sem=core_recv, device_id={"pts": other}, device_id_type=MESH,
    )
    core_copy.start()
    core_copy.wait_recv()
    ring[0] = pair[0] + pair[1]

    def gram_copy(k):
        return pltpu.make_async_remote_copy(
            src_ref=ring.at[0], dst_ref=ring.at[k],
            send_sem=ar_send.at[k], recv_sem=ar_recv.at[k],
            device_id={"pts": lax.rem(s + 2 * k, ns)}, device_id_type=MESH,
        )

    for k in range(1, nz):
        gram_copy(k).start()
    for k in range(1, nz):
        gram_copy(k).wait_recv()
    chip = s // 2
    total = ring[chip]
    for k in range(1, nz):
        total = total + ring[lax.rem(chip - k + nz, nz)]
    total_ref[...] = total
    for q in range(nq):
        row_copy(q).wait()
    for q in range(nq):
        for k in range(1, nt):
            peer_copy(q, k).wait_send()
    core_copy.wait_send()
    for k in range(1, nz):
        gram_copy(k).wait_send()


def finish(total_ref, rows_ref, cross_ref, modes_ref, mix_ref):
    lf = cross_ref.shape[0]

    @pl.when(pl.program_id(0) == 0)
    def _():
        total = [total_ref[:, k * NB:(k + 1) * NB] for k in range(2 * lf)]
        for f in range(lf):
            cross_ref[f, 0] = total[2 * f]
            cross_ref[f, 1] = total[2 * f + 1]
        zs = inverse_roots(
            [normalized(total[2 * f], total[2 * f + 1]) for f in range(lf)]
        )
        roots = []
        for f in range(lf):
            z = zs[f].astype(BF16).astype(F32)
            pieces = []
            if f:
                pieces.append(jnp.zeros((2 * NB, f * 2 * NB), F32))
            pieces.append(z)
            if f < lf - 1:
                pieces.append(jnp.zeros((2 * NB, (lf - 1 - f) * 2 * NB), F32))
            roots.append(jnp.concatenate(pieces, axis=1))
        mix_ref[...] = jnp.concatenate(roots, axis=0).astype(BF16)

    for a in range(0, rows_ref.shape[2], CHUNK):
        cols = pl.ds(a, CHUNK)
        out = jnp.dot(
            mix_ref[...], rows_ref[0, :, cols], preferred_element_type=F32
        )
        modes_ref[:, :, 0, :, cols] = out.astype(BF16).reshape(lf, 2, NB, CHUNK)


def on_device(nt, ns, series, weights, freq_bins):
    table = build_table(freq_bins)
    table = jnp.concatenate([table[:, :HALF], table[:, HALF:]], axis=0)
    points = series.shape[2]
    nq = points // CHUNK + 1
    lb, lf = NB // nt, NF // nt
    rows = NB * 2 * lf
    part = lb * 2 * lf
    vmem = pl.BlockSpec(memory_space=pltpu.VMEM)
    total, x = pl.pallas_call(
        functools.partial(kernel, nt, ns),
        out_shape=(
            jax.ShapeDtypeStruct((NB, 2 * lf * NB), F32),
            jax.ShapeDtypeStruct((3, rows, points), BF16),
        ),
        in_specs=[pl.BlockSpec(memory_space=pl.ANY), vmem, vmem],
        out_specs=(vmem, pl.BlockSpec(memory_space=pl.ANY)),
        scratch_shapes=[
            pltpu.VMEM((3, series.shape[0], points), BF16),
            pltpu.VMEM((nt, 3 * part + 8 * lf, points), BF16),
            pltpu.VMEM((nt, 3 * part + 8 * lf, points), BF16),
            pltpu.VMEM((3, rows, points), BF16),
            pltpu.VMEM((2, NB, 2 * lf * NB), F32),
            pltpu.VMEM((ns // 2, NB, 2 * lf * NB), F32),
            pltpu.SemaphoreType.DMA((nq,)),
            pltpu.SemaphoreType.DMA((nq, nt)),
            pltpu.SemaphoreType.DMA((nq, nt)),
            pltpu.SemaphoreType.DMA,
            pltpu.SemaphoreType.DMA,
            pltpu.SemaphoreType.DMA((ns // 2,)),
            pltpu.SemaphoreType.DMA((ns // 2,)),
            pltpu.SemaphoreType.DMA((nq,)),
        ],
        compiler_params=pltpu.CompilerParams(
            collective_id=0, has_side_effects=True, vmem_limit_bytes=56 * 2**20
        ),
    )(series.transpose(1, 0, 2), table, weights.reshape(1, points))
    cross, modes = pl.pallas_call(
        finish,
        grid=(3,),
        out_shape=(
            jax.ShapeDtypeStruct((lf, 2, NB, NB), F32),
            jax.ShapeDtypeStruct((lf, 2, 3, NB, points), BF16),
        ),
        in_specs=[
            pl.BlockSpec((NB, 2 * lf * NB), lambda c: (0, 0)),
            pl.BlockSpec((1, rows, points), lambda c: (c, 0, 0)),
        ],
        out_specs=(
            pl.BlockSpec((lf, 2, NB, NB), lambda c: (0, 0, 0, 0)),
            pl.BlockSpec((lf, 2, 1, NB, points), lambda c: (0, 0, c, 0, 0)),
        ),
        scratch_shapes=[pltpu.VMEM((rows, rows), BF16)],
        compiler_params=pltpu.CompilerParams(vmem_limit_bytes=56 * 2**20),
    )(total, x)
    return cross, modes.transpose(0, 1, 3, 2, 4)


def solution(mesh):
    nt, ns = mesh.shape["tm"], mesh.shape["pts"]
    in_specs = (P("tm", None, "pts"), P("pts"), P())
    out_specs = (P("tm", None, None, None), P("tm", None, None, None, "pts"))
    return jax.shard_map(
        functools.partial(on_device, nt, ns), mesh=mesh, in_specs=in_specs,
        out_specs=out_specs, check_vma=False
    )
```

profile of v0, /device:TPU:0, one launch (start us, length us, event | category | flops | bytes accessed | tf_op | source)
XLA Modules:
  0.0 42.1 jit_solution(6236949734952238375)
XLA Ops:
  0.7 0.9 %multiply_convert_fusion.1 = (bf16[16,1,512]{2,0,1:T(8,128)(2,1)S(1)}, bf16[16,1,512]{2,0,1:T(8,128)(2,1)S(1)}) fusion(f32[512]{0:T(512)S(1)} %subtract_multiply_fusion, s32[16]{0:T(128)} %param.5), kind=kLoop, calls=%fused_computation.9 | loop fusion | flops 155648 | bytes 34880 | tf_op jit(solution)/shard_map/convert
  1.6 0.6 %pad_maximum_fusion.1.table_ref = bf16[64,256]{1,0:T(8,128)(2,1)} fusion(bf16[32,256]{1,0:T(8,128)(2,1)S(1)} %get-tuple-element.11, bf16[32,256]{1,0:T(8,128)(2,1)S(1)} %get-tuple-element.10), kind=kLoop, calls=%fused_computation.7 | loop fusion | flops 65536 | bytes 65536 | tf_op jit(solution)/shard_map/concatenate | solution.py:269
  2.3 34.1 %shard_map.50 = (f32[32,256]{1,0:T(8,128)}, bf16[3,256,1024]{2,1,0:T(8,128)(2,1)}) custom-call(bf16[3,2048,1024]{2,1,0:T(8,128)(2,1)} %bitcast.3, bf16[64,256]{1,0:T(8,128)(2,1)} %pad_maximum_fusion.1.table_ref, f32[1,1024]{1,0:T(1,128)} %bitcast.4), custom_call_target="tpu_custom_call" | custom-call | tf_op jit(solution)/shard_map/pallas_call | solution.py:276
  36.3 5.7 %shard_map.51 = (f32[4,2,32,32]{3,2,1,0:T(8,128)}, bf16[4,2,3,32,1024]{4,3,2,1,0:T(8,128)(2,1)}) custom-call(f32[32,256]{1,0:T(8,128)} %get-tuple-element.6.total_ref, bf16[3,256,1024]{2,1,0:T(8,128)(2,1)} %get-tuple-element.7.rows_ref), custom_call_target="tpu_custom_call" | custom-call | tf_op jit(solution)/shard_map/pallas_call | solution.py:304
  (5 shorter events, 0.1 us)
where the time goes:
time: 42.4 us; the launch traced here: 42.1 us
  Pallas kernels  39.8 us (94%)
  other arithmetic  1.54 us (4%)
  between operations  0.67 us (2%)
    pallas_call x1, Pallas kernels, on_device(): pl.pallas_call(functools.partial(kernel, nt, ns), out_shape=(jax.ShapeDty...  34.1 us
    pallas_call x1, Pallas kernels, on_device(): pl.pallas_call(finish, grid=(3,), out_shape=(jax.ShapeDtypeStruct((lf, 2,...  5.75 us
    another operation x1, other arithmetic  0.87 us

commit v1 on v0

v1 whole, which is shorter than its diff:
```python
import functools

import jax
import jax.numpy as jnp
from jax import lax
from jax.experimental import pallas as pl
from jax.experimental.pallas import tpu as pltpu
from jax.sharding import PartitionSpec as P

NFFT = 512
NB = 32
NF = 16
ITERS = 4
HALF = NFFT // 2
UNIT = 256
MESH = pl.DeviceIdType.MESH
F32 = jnp.float32
BF16 = jnp.bfloat16


def half_wave(index):
    x = index.astype(F32) * F32(jnp.pi / 512.0)
    x2 = x * x
    c = F32(1.0 / 479001600.0)
    for v in (-1.0 / 3628800.0, 1.0 / 40320.0, -1.0 / 720.0, 1.0 / 24.0, -0.5, 1.0):
        c = c * x2 + F32(v)
    s = F32(-1.0 / 39916800.0)
    for v in (1.0 / 362880.0, -1.0 / 5040.0, 1.0 / 120.0, -1.0 / 6.0, 1.0):
        s = s * x2 + F32(v)
    return c, s * x


def build_table(freq_ref):
    shape = (2 * NF, HALF)
    row = lax.broadcasted_iota(jnp.int32, shape, 0)
    col = lax.broadcasted_iota(jnp.int32, shape, 1)
    freq = jnp.zeros(shape, jnp.int32)
    for f in range(NF):
        freq = jnp.where(row // 2 == f, freq_ref[f], freq)
    halves = []
    for h in range(2):
        n = col + h * HALF
        wc, _ = half_wave(n - HALF)
        window = wc * wc * F32((8.0 / (3.0 * NFFT)) ** 0.5)
        index = ((freq * n) & (NFFT - 1)) - HALF
        c, s = half_wave(index)
        cosine = 2.0 * s * s - 1.0
        minus_sine = 2.0 * s * c
        halves.append(jnp.where(row % 2 == 0, cosine, minus_sine) * window)
    return jnp.concatenate(halves, axis=0).astype(BF16)


def dot(left, right):
    return jnp.dot(left, right, preferred_element_type=F32)


def dot_t(left, right):
    return lax.dot_general(
        left, right, (((1,), (1,)), ((), ())), preferred_element_type=F32
    )


def split(value):
    hi = value.astype(BF16)
    return hi, (value - hi.astype(F32)).astype(BF16)


def dot_split(left, right):
    return dot(left[0], right[0]) + (dot(left[0], right[1]) + dot(left[1], right[0]))


def eye(size):
    row = lax.broadcasted_iota(jnp.int32, (size, size), 0)
    col = lax.broadcasted_iota(jnp.int32, (size, size), 1)
    return (row == col).astype(F32)


def normalized(real, imag):
    norm = jnp.sqrt(jnp.sum(real * real + imag * imag, axis=(0, 1), keepdims=True))
    upper = jnp.concatenate([real, -imag], axis=1)
    lower = jnp.concatenate([imag, real], axis=1)
    return jnp.concatenate([upper, lower], axis=0) * (1.0 / norm)


def inverse_roots(ys):
    half_three = 1.5 * eye(2 * NB)
    zs = None
    for it in range(ITERS):
        if zs is None:
            steps = [half_three - 0.5 * y for y in ys]
            ys = [dot_split(split(y), split(s)) for y, s in zip(ys, steps)]
            zs = steps
            continue
        zsp = [split(z) for z in zs]
        ysp = [split(y) for y in ys]
        steps = [half_three - 0.5 * dot_split(z, y) for z, y in zip(zsp, ysp)]
        ssp = [split(s) for s in steps]
        if it < ITERS - 1:
            ys = [dot_split(y, s) for y, s in zip(ysp, ssp)]
        zs = [dot_split(s, z) for s, z in zip(ssp, zsp)]
    return zs


def kernel(nt, ns, lf, series, freq, weights, cross_ref, modes_ref,
           xbuf, table, wbuf, fbuf, mid, edge, send, land, esend, eland, xall,
           out, ar, in_sem, small_sem, a_send, a_recv, e_send, e_recv,
           g_send, g_recv, out_sem):
    t = lax.axis_index("tm")
    s = lax.axis_index("pts")
    points = xbuf.shape[2]
    nq = points // UNIT
    nu = 3 * nq
    lanes = nu * UNIT
    lb = NB // nt
    per = 2 * lf
    rows = 2 * lb

    def series_copy(u):
        cols = pl.ds(u // 3 * UNIT, UNIT)
        return pltpu.make_async_copy(
            series.at[u % 3, :, cols], xbuf.at[u % 3, :, cols], in_sem.at[u]
        )

    freq_copy = pltpu.make_async_copy(freq, fbuf, small_sem.at[0])
    weight_copy = pltpu.make_async_copy(weights, wbuf, small_sem.at[1])
    freq_copy.start()
    for u in range(nu):
        series_copy(u).start()
    weight_copy.start()
    barrier = pltpu.get_barrier_semaphore()
    for k in range(1, nt):
        pl.semaphore_signal(barrier, inc=1, device_id={"tm": lax.rem(t + k, nt)},
                            device_id_type=MESH)
    for k in range(1, ns):
        pl.semaphore_signal(barrier, inc=1, device_id={"pts": lax.rem(s + k, ns)},
                            device_id_type=MESH)
    freq_copy.wait()
    table[...] = build_table(fbuf)

    early = lf // 2
    pieces = [(0, early, u, 1) for u in range(3)]
    pieces += [(0, early, u, 3) for u in range(3, nu, 3)]
    for f in range(early, lf):
        if f < lf - 1:
            pieces.append((f, 1, 0, nu))
        else:
            pieces += [(f, 1, 0, nu // 2), (f, 1, nu // 2, nu // 4),
                       (f, 1, nu // 2 + nu // 4, nu // 4)]

    def piece_copy(p, k):
        f, nf, u, n = pieces[p]
        to = lax.rem(t + k, nt)
        at = (pl.ds(f * rows, nf * rows), pl.ds(u * UNIT, n * UNIT))
        return pltpu.make_async_remote_copy(
            src_ref=send.at[(to, *at)], dst_ref=land.at[(k, *at)],
            send_sem=a_send.at[p, k], recv_sem=a_recv.at[p, k],
            device_id={"tm": to}, device_id_type=MESH,
        )

    def edge_copy(k):
        to = lax.rem(t + k, nt)
        return pltpu.make_async_remote_copy(
            src_ref=esend.at[to], dst_ref=eland.at[k],
            send_sem=e_send.at[k], recv_sem=e_recv.at[k],
            device_id={"tm": to}, device_id_type=MESH,
        )

    def gram_copy(f, k):
        return pltpu.make_async_remote_copy(
            src_ref=ar.at[f, 0], dst_ref=ar.at[f, k],
            send_sem=g_send.at[f, k], recv_sem=g_recv.at[f, k],
            device_id={"pts": lax.rem(s + k, ns)}, device_id_type=MESH,
        )

    def out_copy(f):
        return pltpu.make_async_copy(out.at[f], modes_ref.at[f], out_sem.at[f])

    def transform(u):
        series_copy(u).wait()
        cols = pl.ds(u // 3 * UNIT, UNIT)
        at = pl.ds(u * UNIT, UNIT)
        first = None
        for j in range(lb):
            both = dot(table[...], xbuf[u % 3, j * HALF:(j + 1) * HALF, cols])
            if j == 0:
                edge[:, at] = both[2 * NF:]
            else:
                value = first + both[2 * NF:]
                for v in range(UNIT // 128):
                    mid[v, pl.ds(j - 1, 2 * NF, stride=lb), :] = value[:, v * 128:(v + 1) * 128]
            first = both[:2 * NF]
        for v in range(UNIT // 128):
            mid[v, pl.ds(lb - 1, 2 * NF, stride=lb), :] = first[:, v * 128:(v + 1) * 128]
        for d in range(nt):
            for v in range(UNIT // 128):
                send[d, :, pl.ds(u * UNIT + v * 128, 128)] = mid[
                    v, d * lf * rows:(d + 1) * lf * rows, :].astype(BF16)
        land[0, :, at] = send[t, :, at]

    p = 0
    for u in range(nu):
        transform(u)
        if u == 0:
            pl.semaphore_wait(barrier, nt - 1 + ns - 1)
        if pieces[p][2] + pieces[p][3] == u + 1:
            for k in range(1, nt):
                piece_copy(p, k).start()
            p += 1
    for d in range(nt):
        e = edge[d * per:(d + 1) * per, :]
        esend[d] = jnp.concatenate([e[:, :lanes // 2], e[:, lanes // 2:]], axis=0).astype(BF16)
    for k in range(1, nt):
        edge_copy(k).start()
    for r in range(p, len(pieces)):
        for k in range(1, nt):
            piece_copy(r, k).start()
    eland[0] = esend[t]
    weight_copy.wait()

    last_row = lax.broadcasted_iota(jnp.int32, (lb, UNIT), 0) == lb - 1

    def unit_rows(f, u):
        at = pl.ds(u * UNIT, UNIT)
        half = u * UNIT // (lanes // 2)
        eat = pl.ds(u * UNIT - half * (lanes // 2), UNIT)
        parts = [[], []]
        for src in range(nt):
            x = land[lax.rem(t - src + nt, nt), f * rows:(f + 1) * rows, at].astype(F32)
            e = eland[lax.rem(t - src - 1 + nt, nt), :, eat].astype(F32)
            for i in range(2):
                r = half * per + 2 * f + i
                tail = jnp.where(last_row, e[r:r + 1], 0.0)
                parts[i].append(x[i * lb:(i + 1) * lb] + tail)
        return jnp.concatenate(parts[0] + parts[1], axis=0).astype(BF16)

    def gram(f, units, total):
        for u in units:
            x = unit_rows(f, u)
            xall[f, :, u * UNIT:(u + 1) * UNIT] = x
            w = wbuf[:, u // 3 * UNIT:(u // 3 + 1) * UNIT]
            xw = (x.astype(F32) * w).astype(BF16)
            part = dot_t(xw, x)
            total = part if total is None else total + part
        return total

    def share(f, pair):
        real = pair[:NB, :NB] + pair[NB:, NB:]
        imag = pair[:NB, NB:] - pair[NB:, :NB]
        h = NB // 2
        packed = jnp.concatenate([real[:h], imag[:h], real[h:], imag[h:]], axis=1)
        ar[f, 0] = packed.astype(BF16)
        for k in range(1, ns):
            gram_copy(f, k).start()

    def collect(f):
        for k in range(1, ns):
            gram_copy(f, k).wait_recv()
        total = None
        for src in range(ns):
            v = ar[f, lax.rem(s - src + ns, ns)].astype(F32)
            total = v if total is None else total + v
        real = jnp.concatenate([total[:, :NB], total[:, 2 * NB:3 * NB]], axis=0)
        imag = jnp.concatenate([total[:, NB:2 * NB], total[:, 3 * NB:]], axis=0)
        cross_ref[f, 0] = real
        cross_ref[f, 1] = imag
        return normalized(real, imag)

    def finish(bins):
        roots = inverse_roots([collect(f) for f in bins])
        for f, root in zip(bins, roots):
            root = root.astype(BF16)
            for u in range(nu):
                y = dot(root, xall[f, :, u * UNIT:(u + 1) * UNIT]).astype(BF16)
                cols = pl.ds(u // 3 * UNIT, UNIT)
                for i in range(2):
                    out[f, i, u % 3, :, cols] = y[i * NB:(i + 1) * NB]
            out_copy(f).start()

    def arrived(p):
        for k in range(1, nt):
            piece_copy(p, k).wait_recv()

    for k in range(1, nt):
        edge_copy(k).wait_recv()
    for r in range(p):
        arrived(r)
    for f in range(early):
        share(f, gram(f, range(nu), None))
    finish(range(early))
    for f in range(early, lf - 1):
        arrived(p)
        p += 1
        share(f, gram(f, range(nu), None))
    total = None
    for r in range(p, len(pieces)):
        arrived(r)
        _, _, u, n = pieces[r]
        total = gram(lf - 1, range(u, u + n), total)
    share(lf - 1, total)
    finish(range(early, lf - 1))
    finish([lf - 1])

    for r in range(len(pieces)):
        for k in range(1, nt):
            piece_copy(r, k).wait_send()
    for k in range(1, nt):
        edge_copy(k).wait_send()
    for f in range(lf):
        for k in range(1, ns):
            gram_copy(f, k).wait_send()
    for f in range(lf):
        out_copy(f).wait()


def on_device(nt, ns, series, weights, freq_bins):
    points = series.shape[2]
    nu = 3 * (points // UNIT)
    lanes = 3 * points
    lb, lf = NB // nt, NF // nt
    rows = 2 * lb
    n_pieces = 3 + nu // 3 - 1 + (lf - lf // 2 - 1) + 3
    hbm = pl.BlockSpec(memory_space=pl.ANY)
    vmem = pl.BlockSpec(memory_space=pltpu.VMEM)
    cross, modes = pl.pallas_call(
        functools.partial(kernel, nt, ns, lf),
        out_shape=(
            jax.ShapeDtypeStruct((lf, 2, NB, NB), F32),
            jax.ShapeDtypeStruct((lf, 2, 3, NB, points), BF16),
        ),
        in_specs=[hbm, hbm, hbm],
        out_specs=(vmem, hbm),
        scratch_shapes=[
            pltpu.VMEM((3, series.shape[0], points), BF16),
            pltpu.VMEM((4 * NF, HALF), BF16),
            pltpu.VMEM((1, points), F32),
            pltpu.SMEM((NF,), jnp.int32),
            pltpu.VMEM((UNIT // 128, 2 * NF * lb, 128), F32),
            pltpu.VMEM((2 * NF, lanes), F32),
            pltpu.VMEM((nt, lf * rows, lanes), BF16),
            pltpu.VMEM((nt, lf * rows, lanes), BF16),
            pltpu.VMEM((nt, 4 * lf, lanes // 2), BF16),
            pltpu.VMEM((nt, 4 * lf, lanes // 2), BF16),
            pltpu.VMEM((lf, 2 * NB, lanes), BF16),
            pltpu.VMEM((lf, 2, 3, NB, points), BF16),
            pltpu.VMEM((lf, ns, NB // 2, 4 * NB), BF16),
            pltpu.SemaphoreType.DMA((nu,)),
            pltpu.SemaphoreType.DMA((2,)),
            pltpu.SemaphoreType.DMA((n_pieces, nt)),
            pltpu.SemaphoreType.DMA((n_pieces, nt)),
            pltpu.SemaphoreType.DMA((nt,)),
            pltpu.SemaphoreType.DMA((nt,)),
            pltpu.SemaphoreType.DMA((lf, ns)),
            pltpu.SemaphoreType.DMA((lf, ns)),
            pltpu.SemaphoreType.DMA((lf,)),
        ],
        compiler_params=pltpu.CompilerParams(
            collective_id=0, has_side_effects=True, vmem_limit_bytes=54 * 2**20
        ),
    )(series.transpose(1, 0, 2), freq_bins, weights.reshape(1, points))
    return cross, modes.transpose(0, 1, 3, 2, 4)


def solution(mesh):
    nt, ns = mesh.shape["tm"], mesh.shape["pts"]
    in_specs = (P("tm", None, "pts"), P("pts"), P())
    out_specs = (P("tm", None, None, None), P("tm", None, None, None, "pts"))
    return jax.shard_map(
        functools.partial(on_device, nt, ns), mesh=mesh, in_specs=in_specs,
        out_specs=out_specs, check_vma=False
    )
```

time: 42.4 us -> 40.6 us (0.958)
  Pallas kernels: 39.8 us -> 35.5 us
  local copies, waits for them, and re-layouts: 0.06 us -> 4.31 us
  other arithmetic: 1.54 us -> 0 us
    pallas_call x2 -> x1, Pallas kernels: 39.8 us -> 35.5 us  [on_device(): pl.pallas_call(functools.partial(kernel, nt, ns, lf), out_shape=(jax.Shap...]
    unnamed x0 -> x2, local copies, waits for them, and re-layouts: none -> 4.31 us
    another operation x2 -> x0, other arithmetic: 0.88 us -> none
    concatenate x1 -> x0, other arithmetic: 0.62 us -> none  [on_device(): table = jnp.concatenate([table[:, :HALF], table[:, HALF:]], axis=0)]
where the time goes in v1:
time: 40.6 us; the launch traced here: 40.4 us
  Pallas kernels  35.5 us (87%)
  local copies, waits for them, and re-layouts  4.31 us (11%)
  between operations  0.64 us (2%)
    pallas_call x1, Pallas kernels, on_device(): pl.pallas_call(functools.partial(kernel, nt, ns, lf), out_shape=(jax.Shap...  35.5 us
    unnamed x2, local copies, waits for them, and re-layouts  4.31 us

profile of v1, /device:TPU:0, one launch (start us, length us, event | category | flops | bytes accessed | tf_op | source)
XLA Modules:
  0.0 40.4 jit_solution(2499507320621043533)
XLA Ops:
  0.6 35.5 %shard_map.50 = (f32[4,2,32,32]{3,2,1,0:T(8,128)}, bf16[4,2,3,32,1024]{4,3,2,1,0:T(8,128)(2,1)}) custom-call(bf16[3,2048,1024]{2,1,0:T(8,128)(2,1)} %bitcast.3, s32[16]{0:T(128)} %freq.1, f32[1,1024]{1,0:T(1,128)} %bitcast.5), custom_call_target="tpu_custom_call" | custom-call | tf_op jit(solution)/shard_map/pallas_call | solution.py:324
  36.1 1.6 %copy.7 = f32[4,2,32,32]{3,2,1,0:T(8,128)} copy(f32[4,2,32,32]{3,2,1,0:T(8,128)} %get-tuple-element.8) | data formatting | bytes 65536
  37.7 2.7 %copy.8 = bf16[4,2,32,3,1024]{4,2,3,1,0:T(8,128)(2,1)} copy(bf16[4,2,32,3,1024]{4,2,3,1,0:T(8,128)(2,1)} %bitcast.4) | data formatting | bytes 3145728

commit v2 on v1

--- a/solution.py
+++ b/solution.py
@@ -101,10 +101,37 @@
     return zs
 
 
-def kernel(nt, ns, lf, series, freq, weights, cross_ref, modes_ref,
+def mix(root, rows_of, out, nu):
+    for u in range(nu):
+        y = dot(root, rows_of(u)).astype(BF16)
+        cols = pl.ds(u // 3 * UNIT, UNIT)
+        for i in range(2):
+            out[i, u % 3, :, cols] = y[i * NB:(i + 1) * NB]
+
+
+def finish_kernel(nu, cross_in, early, x, cross_ref, modes_ref,
+                  out, early_sem, out_sem):
+    lf = cross_in.shape[0]
+    copies = [
+        pltpu.make_async_copy(early.at[f], modes_ref.at[f], early_sem.at[f])
+        for f in range(lf - 1)
+    ]
+    for c in copies:
+        c.start()
+    cross_ref[...] = cross_in[...]
+    y = normalized(cross_in[lf - 1, 0], cross_in[lf - 1, 1])
+    (root,) = inverse_roots([y])
+    mix(root.astype(BF16), lambda u: x[:, u * UNIT:(u + 1) * UNIT], out, nu)
+    copies.append(pltpu.make_async_copy(out, modes_ref.at[lf - 1], out_sem))
+    copies[-1].start()
+    for c in copies:
+        c.wait()
+
+
+def kernel(nt, ns, lf, series, freq, weights, cross_ref, early_ref, x_ref,
            xbuf, table, wbuf, fbuf, mid, edge, send, land, esend, eland, xall,
-           out, ar, in_sem, small_sem, a_send, a_recv, e_send, e_recv,
-           g_send, g_recv, out_sem):
+           ar, in_sem, small_sem, a_send, a_recv, e_send, e_recv,
+           g_send, g_recv):
     t = lax.axis_index("tm")
     s = lax.axis_index("pts")
     points = xbuf.shape[2]
@@ -124,9 +151,8 @@
     freq_copy = pltpu.make_async_copy(freq, fbuf, small_sem.at[0])
     weight_copy = pltpu.make_async_copy(weights, wbuf, small_sem.at[1])
     freq_copy.start()
-    for u in range(nu):
+    for u in range(3):
         series_copy(u).start()
-    weight_copy.start()
     barrier = pltpu.get_barrier_semaphore()
     for k in range(1, nt):
         pl.semaphore_signal(barrier, inc=1, device_id={"tm": lax.rem(t + k, nt)},
@@ -134,6 +160,9 @@
     for k in range(1, ns):
         pl.semaphore_signal(barrier, inc=1, device_id={"pts": lax.rem(s + k, ns)},
                             device_id_type=MESH)
+    for u in range(3, nu):
+        series_copy(u).start()
+    weight_copy.start()
     freq_copy.wait()
     table[...] = build_table(fbuf)
 
@@ -172,8 +201,8 @@
             device_id={"pts": lax.rem(s + k, ns)}, device_id_type=MESH,
         )
 
-    def out_copy(f):
-        return pltpu.make_async_copy(out.at[f], modes_ref.at[f], out_sem.at[f])
+    def rows_of(f):
+        return xall.at[f] if f < lf - 1 else x_ref
 
     def transform(u):
         series_copy(u).wait()
@@ -211,9 +240,11 @@
         esend[d] = jnp.concatenate([e[:, :lanes // 2], e[:, lanes // 2:]], axis=0).astype(BF16)
     for k in range(1, nt):
         edge_copy(k).start()
-    for r in range(p, len(pieces)):
+    def begin(r):
         for k in range(1, nt):
             piece_copy(r, k).start()
+
+    begin(p)
     eland[0] = esend[t]
     weight_copy.wait()
 
@@ -236,7 +267,7 @@
     def gram(f, units, total):
         for u in units:
             x = unit_rows(f, u)
-            xall[f, :, u * UNIT:(u + 1) * UNIT] = x
+            rows_of(f)[:, u * UNIT:(u + 1) * UNIT] = x
             w = wbuf[:, u // 3 * UNIT:(u // 3 + 1) * UNIT]
             xw = (x.astype(F32) * w).astype(BF16)
             part = dot_t(xw, x)
@@ -263,18 +294,13 @@
         imag = jnp.concatenate([total[:, NB:2 * NB], total[:, 3 * NB:]], axis=0)
         cross_ref[f, 0] = real
         cross_ref[f, 1] = imag
-        return normalized(real, imag)
+        return real, imag
 
     def finish(bins):
-        roots = inverse_roots([collect(f) for f in bins])
+        roots = inverse_roots([normalized(*collect(f)) for f in bins])
         for f, root in zip(bins, roots):
-            root = root.astype(BF16)
-            for u in range(nu):
-                y = dot(root, xall[f, :, u * UNIT:(u + 1) * UNIT]).astype(BF16)
-                cols = pl.ds(u // 3 * UNIT, UNIT)
-                for i in range(2):
-                    out[f, i, u % 3, :, cols] = y[i * NB:(i + 1) * NB]
-            out_copy(f).start()
+            mix(root.astype(BF16), lambda u: xall[f, :, u * UNIT:(u + 1) * UNIT],
+                early_ref.at[f], nu)
 
     def arrived(p):
         for k in range(1, nt):
@@ -286,11 +312,16 @@
         arrived(r)
     for f in range(early):
         share(f, gram(f, range(nu), None))
-    finish(range(early))
+    begin(p + 1)
     for f in range(early, lf - 1):
         arrived(p)
         p += 1
         share(f, gram(f, range(nu), None))
+        if f < lf - 2:
+            begin(p + 1)
+    for r in range(p + 1, len(pieces)):
+        begin(r)
+    finish(range(early))
     total = None
     for r in range(p, len(pieces)):
         arrived(r)
@@ -298,7 +329,7 @@
         total = gram(lf - 1, range(u, u + n), total)
     share(lf - 1, total)
     finish(range(early, lf - 1))
-    finish([lf - 1])
+    collect(lf - 1)
 
     for r in range(len(pieces)):
         for k in range(1, nt):
@@ -308,8 +339,6 @@
     for f in range(lf):
         for k in range(1, ns):
             gram_copy(f, k).wait_send()
-    for f in range(lf):
-        out_copy(f).wait()
 
 
 def on_device(nt, ns, series, weights, freq_bins):
@@ -321,14 +350,15 @@
     n_pieces = 3 + nu // 3 - 1 + (lf - lf // 2 - 1) + 3
     hbm = pl.BlockSpec(memory_space=pl.ANY)
     vmem = pl.BlockSpec(memory_space=pltpu.VMEM)
-    cross, modes = pl.pallas_call(
+    cross, early, x = pl.pallas_call(
         functools.partial(kernel, nt, ns, lf),
         out_shape=(
             jax.ShapeDtypeStruct((lf, 2, NB, NB), F32),
-            jax.ShapeDtypeStruct((lf, 2, 3, NB, points), BF16),
+            jax.ShapeDtypeStruct((lf - 1, 2, 3, NB, points), BF16),
+            jax.ShapeDtypeStruct((2 * NB, lanes), BF16),
         ),
         in_specs=[hbm, hbm, hbm],
-        out_specs=(vmem, hbm),
+        out_specs=(vmem, vmem, vmem),
         scratch_shapes=[
             pltpu.VMEM((3, series.shape[0], points), BF16),
             pltpu.VMEM((4 * NF, HALF), BF16),
@@ -340,8 +370,7 @@
             pltpu.VMEM((nt, lf * rows, lanes), BF16),
             pltpu.VMEM((nt, 4 * lf, lanes // 2), BF16),
             pltpu.VMEM((nt, 4 * lf, lanes // 2), BF16),
-            pltpu.VMEM((lf, 2 * NB, lanes), BF16),
-            pltpu.VMEM((lf, 2, 3, NB, points), BF16),
+            pltpu.VMEM((lf - 1, 2 * NB, lanes), BF16),
             pltpu.VMEM((lf, ns, NB // 2, 4 * NB), BF16),
             pltpu.SemaphoreType.DMA((nu,)),
             pltpu.SemaphoreType.DMA((2,)),
@@ -351,12 +380,27 @@
             pltpu.SemaphoreType.DMA((nt,)),
             pltpu.SemaphoreType.DMA((lf, ns)),
             pltpu.SemaphoreType.DMA((lf, ns)),
-            pltpu.SemaphoreType.DMA((lf,)),
         ],
         compiler_params=pltpu.CompilerParams(
-            collective_id=0, has_side_effects=True, vmem_limit_bytes=54 * 2**20
+            collective_id=0, has_side_effects=True, vmem_limit_bytes=50 * 2**20
         ),
-    )(series.transpose(1, 0, 2), freq_bins, weights.reshape(1, points))
+    )(*(pltpu.with_memory_space_constraint(v, pltpu.HBM)
+        for v in (series.transpose(1, 0, 2), freq_bins, weights.reshape(1, points))))
+    cross, modes = pl.pallas_call(
+        functools.partial(finish_kernel, nu),
+        out_shape=(
+            jax.ShapeDtypeStruct((lf, 2, NB, NB), F32),
+            jax.ShapeDtypeStruct((lf, 2, 3, NB, points), BF16),
+        ),
+        in_specs=[vmem, vmem, vmem],
+        out_specs=(vmem, hbm),
+        scratch_shapes=[
+            pltpu.VMEM((2, 3, NB, points), BF16),
+            pltpu.SemaphoreType.DMA((lf - 1,)),
+            pltpu.SemaphoreType.DMA,
+        ],
+        compiler_params=pltpu.CompilerParams(vmem_limit_bytes=16 * 2**20),
+    )(cross, early, x)
     return cross, modes.transpose(0, 1, 3, 2, 4)
 
 

time: 40.6 us -> 36.9 us (0.909)
  local copies, waits for them, and re-layouts: 4.31 us -> 0 us
  Pallas kernels: 35.5 us -> 36.1 us
    unnamed x2 -> x0, local copies, waits for them, and re-layouts: 4.31 us -> none
    pallas_call x0 -> x1, Pallas kernels: none -> 2.85 us  [on_device(): pl.pallas_call(functools.partial(finish_kernel, nu), out_shape=(jax.Shape...]
    pallas_call x1, Pallas kernels: 35.5 us -> 33.3 us  [on_device(): pl.pallas_call(functools.partial(kernel, nt, ns, lf), out_shape=(jax.Shap...]
where the time goes in v2:
time: 36.9 us; the launch traced here: 36.8 us
  Pallas kernels  36.1 us (98%)
  between operations  0.64 us (2%)
    pallas_call x1, Pallas kernels, on_device(): pl.pallas_call(functools.partial(kernel, nt, ns, lf), out_shape=(jax.Shap...  33.3 us
    pallas_call x1, Pallas kernels, on_device(): pl.pallas_call(functools.partial(finish_kernel, nu), out_shape=(jax.Shape...  2.85 us

profile of v2, /device:TPU:0, one launch (start us, length us, event | category | flops | bytes accessed | tf_op | source)
XLA Modules:
  0.0 36.8 jit_solution(8636212231666228499)
XLA Ops:
  0.6 33.3 %shard_map.50 = (f32[4,2,32,32]{3,2,1,0:T(8,128)S(1)}, bf16[3,2,3,32,1024]{4,3,2,1,0:T(8,128)(2,1)S(1)}, bf16[64,3072]{1,0:T(8,128)(2,1)S(1)}) custom-call(bf16[3,2048,1024]{2,1,0:T(8,128)(2,1)} %bitcast.3, s32[16]{0:T(128)} %freq.1, f32[1,1024]{1,0:T(1,128)} %bitcast.4), custom_call_target="tpu_custom_call" | custom-call | tf_op jit(solution)/shard_map/pallas_call | solution.py:353
  33.9 2.9 %shard_map.51 = (f32[4,2,32,32]{3,2,1,0:T(8,128)}, bf16[4,2,3,32,1024]{4,3,2,1,0:T(8,128)(2,1)}) custom-call(f32[4,2,32,32]{3,2,1,0:T(8,128)S(1)} %get-tuple-element.7.cross_in, bf16[3,2,3,32,1024]{4,3,2,1,0:T(8,128)(2,1)S(1)} %get-tuple-element.8.early, bf16[64,3072]{1,0:T(8,128)(2,1)S(1)} %get-tuple-element.9.x), custom_call_target="tpu_custom_call" | custom-call | tf_op jit(solution)/shard_map/pallas_call | solution.py:389

commit v3 on v2

--- a/solution.py
+++ b/solution.py
@@ -110,15 +110,15 @@
 
 
 def finish_kernel(nu, cross_in, early, x, cross_ref, modes_ref,
-                  out, early_sem, out_sem):
+                  out, early_sem, out_sem, cross_sem):
     lf = cross_in.shape[0]
-    copies = [
+    copies = [pltpu.make_async_copy(cross_in, cross_ref, cross_sem)]
+    copies += [
         pltpu.make_async_copy(early.at[f], modes_ref.at[f], early_sem.at[f])
         for f in range(lf - 1)
     ]
     for c in copies:
         c.start()
-    cross_ref[...] = cross_in[...]
     y = normalized(cross_in[lf - 1, 0], cross_in[lf - 1, 1])
     (root,) = inverse_roots([y])
     mix(root.astype(BF16), lambda u: x[:, u * UNIT:(u + 1) * UNIT], out, nu)
@@ -131,7 +131,7 @@
 def kernel(nt, ns, lf, series, freq, weights, cross_ref, early_ref, x_ref,
            xbuf, table, wbuf, fbuf, mid, edge, send, land, esend, eland, xall,
            ar, in_sem, small_sem, a_send, a_recv, e_send, e_recv,
-           g_send, g_recv):
+           g_send, g_recv, go_sem):
     t = lax.axis_index("tm")
     s = lax.axis_index("pts")
     points = xbuf.shape[2]
@@ -157,9 +157,12 @@
     for k in range(1, nt):
         pl.semaphore_signal(barrier, inc=1, device_id={"tm": lax.rem(t + k, nt)},
                             device_id_type=MESH)
-    for k in range(1, ns):
-        pl.semaphore_signal(barrier, inc=1, device_id={"pts": lax.rem(s + k, ns)},
-                            device_id_type=MESH)
+    root = ns // 2
+
+    @pl.when(s != root)
+    def _():
+        pl.semaphore_signal(barrier, inc=1, device_id={"pts": root}, device_id_type=MESH)
+
     for u in range(3, nu):
         series_copy(u).start()
     weight_copy.start()
@@ -173,8 +176,7 @@
         if f < lf - 1:
             pieces.append((f, 1, 0, nu))
         else:
-            pieces += [(f, 1, 0, nu // 2), (f, 1, nu // 2, nu // 4),
-                       (f, 1, nu // 2 + nu // 4, nu // 4)]
+            pieces += [(f, 1, 0, nu - nu // 4), (f, 1, nu - nu // 4, nu // 4)]
 
     def piece_copy(p, k):
         f, nf, u, n = pieces[p]
@@ -230,7 +232,13 @@
     for u in range(nu):
         transform(u)
         if u == 0:
-            pl.semaphore_wait(barrier, nt - 1 + ns - 1)
+            pl.semaphore_wait(barrier, nt - 1 + jnp.where(s == root, ns - 1, 0))
+
+            @pl.when(s == root)
+            def _():
+                for k in range(1, ns):
+                    pl.semaphore_signal(go_sem, inc=1, device_id={"pts": lax.rem(s + k, ns)},
+                                        device_id_type=MESH)
         if pieces[p][2] + pieces[p][3] == u + 1:
             for k in range(1, nt):
                 piece_copy(p, k).start()
@@ -310,8 +318,14 @@
         edge_copy(k).wait_recv()
     for r in range(p):
         arrived(r)
+    grams = [gram(f, range(nu), None) for f in range(early)]
+
+    @pl.when(s != root)
+    def _():
+        pl.semaphore_wait(go_sem, 1)
+
     for f in range(early):
-        share(f, gram(f, range(nu), None))
+        share(f, grams[f])
     begin(p + 1)
     for f in range(early, lf - 1):
         arrived(p)
@@ -347,7 +361,7 @@
     lanes = 3 * points
     lb, lf = NB // nt, NF // nt
     rows = 2 * lb
-    n_pieces = 3 + nu // 3 - 1 + (lf - lf // 2 - 1) + 3
+    n_pieces = 3 + nu // 3 - 1 + (lf - lf // 2 - 1) + 2
     hbm = pl.BlockSpec(memory_space=pl.ANY)
     vmem = pl.BlockSpec(memory_space=pltpu.VMEM)
     cross, early, x = pl.pallas_call(
@@ -380,6 +394,7 @@
             pltpu.SemaphoreType.DMA((nt,)),
             pltpu.SemaphoreType.DMA((lf, ns)),
             pltpu.SemaphoreType.DMA((lf, ns)),
+            pltpu.SemaphoreType.REGULAR,
         ],
         compiler_params=pltpu.CompilerParams(
             collective_id=0, has_side_effects=True, vmem_limit_bytes=50 * 2**20
@@ -393,10 +408,11 @@
             jax.ShapeDtypeStruct((lf, 2, 3, NB, points), BF16),
         ),
         in_specs=[vmem, vmem, vmem],
-        out_specs=(vmem, hbm),
+        out_specs=(hbm, hbm),
         scratch_shapes=[
             pltpu.VMEM((2, 3, NB, points), BF16),
             pltpu.SemaphoreType.DMA((lf - 1,)),
+            pltpu.SemaphoreType.DMA,
             pltpu.SemaphoreType.DMA,
         ],
         compiler_params=pltpu.CompilerParams(vmem_limit_bytes=16 * 2**20),

time: 36.9 us -> 35.7 us (0.967)
  Pallas kernels: 36.1 us -> 34.9 us
    pallas_call x1, Pallas kernels: 2.85 us -> 2.22 us  [on_device(): pl.pallas_call(functools.partial(finish_kernel, nu), out_shape=(jax.Shape...]
    pallas_call x1, Pallas kernels: 33.3 us -> 32.7 us  [on_device(): pl.pallas_call(functools.partial(kernel, nt, ns, lf), out_shape=(jax.Shap...]
where the time goes in v3:
time: 35.7 us; the launch traced here: 35.5 us
  Pallas kernels  34.9 us (98%)
  between operations  0.64 us (2%)
    pallas_call x1, Pallas kernels, on_device(): pl.pallas_call(functools.partial(kernel, nt, ns, lf), out_shape=(jax.Shap...  32.7 us
    pallas_call x1, Pallas kernels, on_device(): pl.pallas_call(functools.partial(finish_kernel, nu), out_shape=(jax.Shape...  2.22 us

profile of v3, /device:TPU:0, one launch (start us, length us, event | category | flops | bytes accessed | tf_op | source)
XLA Modules:
  0.0 35.5 jit_solution(5183709691232605762)
XLA Ops:
  0.6 32.7 %shard_map.50 = (f32[4,2,32,32]{3,2,1,0:T(8,128)S(1)}, bf16[3,2,3,32,1024]{4,3,2,1,0:T(8,128)(2,1)S(1)}, bf16[64,3072]{1,0:T(8,128)(2,1)S(1)}) custom-call(bf16[3,2048,1024]{2,1,0:T(8,128)(2,1)} %bitcast.3, s32[16]{0:T(128)} %freq.1, f32[1,1024]{1,0:T(1,128)} %bitcast.4), custom_call_target="tpu_custom_call" | custom-call | tf_op jit(solution)/shard_map/pallas_call | solution.py:367
  33.3 2.2 %shard_map.51 = (f32[4,2,32,32]{3,2,1,0:T(8,128)}, bf16[4,2,3,32,1024]{4,3,2,1,0:T(8,128)(2,1)}) custom-call(f32[4,2,32,32]{3,2,1,0:T(8,128)S(1)} %get-tuple-element.7.cross_in, bf16[3,2,3,32,1024]{4,3,2,1,0:T(8,128)(2,1)S(1)} %get-tuple-element.8.early, bf16[64,3072]{1,0:T(8,128)(2,1)S(1)} %get-tuple-element.9.x), custom_call_target="tpu_custom_call" | custom-call | tf_op jit(solution)/shard_map/pallas_call | solution.py:404

commit v4 on v3

--- a/solution.py
+++ b/solution.py
@@ -113,10 +113,8 @@
                   out, early_sem, out_sem, cross_sem):
     lf = cross_in.shape[0]
     copies = [pltpu.make_async_copy(cross_in, cross_ref, cross_sem)]
-    copies += [
-        pltpu.make_async_copy(early.at[f], modes_ref.at[f], early_sem.at[f])
-        for f in range(lf - 1)
-    ]
+    copies.append(
+        pltpu.make_async_copy(early, modes_ref.at[pl.ds(0, lf - 1)], early_sem))
     for c in copies:
         c.start()
     y = normalized(cross_in[lf - 1, 0], cross_in[lf - 1, 1])
@@ -130,8 +128,7 @@
 
 def kernel(nt, ns, lf, series, freq, weights, cross_ref, early_ref, x_ref,
            xbuf, table, wbuf, fbuf, mid, edge, send, land, esend, eland, xall,
-           ar, in_sem, small_sem, a_send, a_recv, e_send, e_recv,
-           g_send, g_recv, go_sem):
+           ar, in_sem, small_sem, send_sem, a_recv, e_recv, g_recv, go_sem):
     t = lax.axis_index("tm")
     s = lax.axis_index("pts")
     points = xbuf.shape[2]
@@ -142,11 +139,12 @@
     per = 2 * lf
     rows = 2 * lb
 
-    def series_copy(u):
-        cols = pl.ds(u // 3 * UNIT, UNIT)
-        return pltpu.make_async_copy(
-            series.at[u % 3, :, cols], xbuf.at[u % 3, :, cols], in_sem.at[u]
-        )
+    loads = [(u, 1) for u in range(3)] + [(u, 3) for u in range(3, nu, 3)]
+
+    def series_copy(i):
+        u, n = loads[i]
+        at = (pl.ds(u % 3, n), slice(None), pl.ds(u // 3 * UNIT, UNIT))
+        return pltpu.make_async_copy(series.at[at], xbuf.at[at], in_sem.at[i])
 
     freq_copy = pltpu.make_async_copy(freq, fbuf, small_sem.at[0])
     weight_copy = pltpu.make_async_copy(weights, wbuf, small_sem.at[1])
@@ -163,8 +161,8 @@
     def _():
         pl.semaphore_signal(barrier, inc=1, device_id={"pts": root}, device_id_type=MESH)
 
-    for u in range(3, nu):
-        series_copy(u).start()
+    for i in range(3, len(loads)):
+        series_copy(i).start()
     weight_copy.start()
     freq_copy.wait()
     table[...] = build_table(fbuf)
@@ -178,13 +176,30 @@
         else:
             pieces += [(f, 1, 0, nu - nu // 4), (f, 1, nu - nu // 4, nu // 4)]
 
+    n_early = nu // 3 + 2
+    pts_peer = {"pts": lax.rem(s + 1, ns)}
+    tm_peer = {"tm": lax.rem(t + 1, nt)}
+
+    def group(source, target, at, send_at, recv, peer):
+        return pltpu.make_async_remote_copy(
+            src_ref=source.at[at], dst_ref=target.at[at], send_sem=send_sem.at[send_at],
+            recv_sem=recv, device_id=peer, device_id_type=MESH,
+        )
+
+    def stage(r):
+        f, nf, u, n = pieces[n_early - 1 + r]
+        if r == 0:
+            u, n = 0, nu
+        at = (pl.ds(1, nt - 1), pl.ds(f * rows, nf * rows), pl.ds(u * UNIT, n * UNIT))
+        return group(land, land, at, 0, a_recv.at[r], tm_peer)
+
     def piece_copy(p, k):
         f, nf, u, n = pieces[p]
         to = lax.rem(t + k, nt)
         at = (pl.ds(f * rows, nf * rows), pl.ds(u * UNIT, n * UNIT))
         return pltpu.make_async_remote_copy(
             src_ref=send.at[(to, *at)], dst_ref=land.at[(k, *at)],
-            send_sem=a_send.at[p, k], recv_sem=a_recv.at[p, k],
+            send_sem=send_sem.at[0], recv_sem=a_recv.at[max(0, p - n_early + 1)],
             device_id={"tm": to}, device_id_type=MESH,
         )
 
@@ -192,14 +207,14 @@
         to = lax.rem(t + k, nt)
         return pltpu.make_async_remote_copy(
             src_ref=esend.at[to], dst_ref=eland.at[k],
-            send_sem=e_send.at[k], recv_sem=e_recv.at[k],
+            send_sem=send_sem.at[1], recv_sem=e_recv,
             device_id={"tm": to}, device_id_type=MESH,
         )
 
     def gram_copy(f, k):
         return pltpu.make_async_remote_copy(
             src_ref=ar.at[f, 0], dst_ref=ar.at[f, k],
-            send_sem=g_send.at[f, k], recv_sem=g_recv.at[f, k],
+            send_sem=send_sem.at[2], recv_sem=g_recv.at[f],
             device_id={"pts": lax.rem(s + k, ns)}, device_id_type=MESH,
         )
 
@@ -207,7 +222,9 @@
         return xall.at[f] if f < lf - 1 else x_ref
 
     def transform(u):
-        series_copy(u).wait()
+        for i, (first_unit, _) in enumerate(loads):
+            if first_unit == u:
+                series_copy(i).wait()
         cols = pl.ds(u // 3 * UNIT, UNIT)
         at = pl.ds(u * UNIT, UNIT)
         first = None
@@ -292,8 +309,8 @@
             gram_copy(f, k).start()
 
     def collect(f):
-        for k in range(1, ns):
-            gram_copy(f, k).wait_recv()
+        at = (f, pl.ds(1, ns - 1))
+        group(ar, ar, at, 2, g_recv.at[f], pts_peer).wait_recv()
         total = None
         for src in range(ns):
             v = ar[f, lax.rem(s - src + ns, ns)].astype(F32)
@@ -311,13 +328,11 @@
                 early_ref.at[f], nu)
 
     def arrived(p):
-        for k in range(1, nt):
-            piece_copy(p, k).wait_recv()
-
-    for k in range(1, nt):
-        edge_copy(k).wait_recv()
-    for r in range(p):
-        arrived(r)
+        stage(p - n_early + 1).wait_recv()
+
+    edges = group(eland, eland, pl.ds(1, nt - 1), 1, e_recv, tm_peer)
+    edges.wait_recv()
+    stage(0).wait_recv()
     grams = [gram(f, range(nu), None) for f in range(early)]
 
     @pl.when(s != root)
@@ -345,14 +360,9 @@
     finish(range(early, lf - 1))
     collect(lf - 1)
 
-    for r in range(len(pieces)):
-        for k in range(1, nt):
-            piece_copy(r, k).wait_send()
-    for k in range(1, nt):
-        edge_copy(k).wait_send()
-    for f in range(lf):
-        for k in range(1, ns):
-            gram_copy(f, k).wait_send()
+    group(send, send, pl.ds(0, nt - 1), 0, a_recv.at[0], tm_peer).wait_send()
+    edges.wait_send()
+    group(ar, ar, (slice(None), pl.ds(1, ns - 1)), 2, g_recv.at[0], pts_peer).wait_send()
 
 
 def on_device(nt, ns, series, weights, freq_bins):
@@ -361,7 +371,6 @@
     lanes = 3 * points
     lb, lf = NB // nt, NF // nt
     rows = 2 * lb
-    n_pieces = 3 + nu // 3 - 1 + (lf - lf // 2 - 1) + 2
     hbm = pl.BlockSpec(memory_space=pl.ANY)
     vmem = pl.BlockSpec(memory_space=pltpu.VMEM)
     cross, early, x = pl.pallas_call(
@@ -386,14 +395,12 @@
             pltpu.VMEM((nt, 4 * lf, lanes // 2), BF16),
             pltpu.VMEM((lf - 1, 2 * NB, lanes), BF16),
             pltpu.VMEM((lf, ns, NB // 2, 4 * NB), BF16),
-            pltpu.SemaphoreType.DMA((nu,)),
+            pltpu.SemaphoreType.DMA((nu // 3 + 2,)),
             pltpu.SemaphoreType.DMA((2,)),
-            pltpu.SemaphoreType.DMA((n_pieces, nt)),
-            pltpu.SemaphoreType.DMA((n_pieces, nt)),
-            pltpu.SemaphoreType.DMA((nt,)),
-            pltpu.SemaphoreType.DMA((nt,)),
-            pltpu.SemaphoreType.DMA((lf, ns)),
-            pltpu.SemaphoreType.DMA((lf, ns)),
+            pltpu.SemaphoreType.DMA((3,)),
+            pltpu.SemaphoreType.DMA((lf - lf // 2 + 2,)),
+            pltpu.SemaphoreType.DMA,
+            pltpu.SemaphoreType.DMA((lf,)),
             pltpu.SemaphoreType.REGULAR,
         ],
         compiler_params=pltpu.CompilerParams(
@@ -411,7 +418,7 @@
         out_specs=(hbm, hbm),
         scratch_shapes=[
             pltpu.VMEM((2, 3, NB, points), BF16),
-            pltpu.SemaphoreType.DMA((lf - 1,)),
+            pltpu.SemaphoreType.DMA,
             pltpu.SemaphoreType.DMA,
             pltpu.SemaphoreType.DMA,
         ],

time: 35.7 us -> 34 us (0.952)
  Pallas kernels: 34.9 us -> 33.2 us
    pallas_call x1, Pallas kernels: 32.7 us -> 31 us  [on_device(): pl.pallas_call(functools.partial(kernel, nt, ns, lf), out_shape=(jax.Shap...]
where the time goes in v4:
time: 34 us; the launch traced here: 33.8 us
  Pallas kernels  33.2 us (98%)
  between operations  0.64 us (2%)
    pallas_call x1, Pallas kernels, on_device(): pl.pallas_call(functools.partial(kernel, nt, ns, lf), out_shape=(jax.Shap...  31 us
    pallas_call x1, Pallas kernels, on_device(): pl.pallas_call(functools.partial(finish_kernel, nu), out_shape=(jax.Shape...  2.18 us

profile of v4, /device:TPU:0, one launch (start us, length us, event | category | flops | bytes accessed | tf_op | source)
XLA Modules:
  0.0 33.8 jit_solution(6302419321160969599)
XLA Ops:
  0.6 31.0 %shard_map.50 = (f32[4,2,32,32]{3,2,1,0:T(8,128)S(1)}, bf16[3,2,3,32,1024]{4,3,2,1,0:T(8,128)(2,1)S(1)}, bf16[64,3072]{1,0:T(8,128)(2,1)S(1)}) custom-call(bf16[3,2048,1024]{2,1,0:T(8,128)(2,1)} %bitcast.3, s32[16]{0:T(128)} %freq.1, f32[1,1024]{1,0:T(1,128)} %bitcast.4), custom_call_target="tpu_custom_call" | custom-call | tf_op jit(solution)/shard_map/pallas_call | solution.py:376
  31.7 2.2 %shard_map.51 = (f32[4,2,32,32]{3,2,1,0:T(8,128)}, bf16[4,2,3,32,1024]{4,3,2,1,0:T(8,128)(2,1)}) custom-call(f32[4,2,32,32]{3,2,1,0:T(8,128)S(1)} %get-tuple-element.7.cross_in, bf16[3,2,3,32,1024]{4,3,2,1,0:T(8,128)(2,1)S(1)} %get-tuple-element.8.early, bf16[64,3072]{1,0:T(8,128)(2,1)S(1)} %get-tuple-element.9.x), custom_call_target="tpu_custom_call" | custom-call | tf_op jit(solution)/shard_map/pallas_call | solution.py:411

commit v5 on v4

--- a/solution.py
+++ b/solution.py
@@ -10,7 +10,6 @@
 NFFT = 512
 NB = 32
 NF = 16
-ITERS = 4
 HALF = NFFT // 2
 UNIT = 256
 MESH = pl.DeviceIdType.MESH
@@ -82,27 +81,29 @@
     return jnp.concatenate([upper, lower], axis=0) * (1.0 / norm)
 
 
-def inverse_roots(ys):
-    half_three = 1.5 * eye(2 * NB)
-    zs = None
-    for it in range(ITERS):
-        if zs is None:
-            steps = [half_three - 0.5 * y for y in ys]
-            ys = [dot_split(split(y), split(s)) for y, s in zip(ys, steps)]
-            zs = steps
-            continue
-        zsp = [split(z) for z in zs]
-        ysp = [split(y) for y in ys]
-        steps = [half_three - 0.5 * dot_split(z, y) for z, y in zip(zsp, ysp)]
-        ssp = [split(s) for s in steps]
-        if it < ITERS - 1:
-            ys = [dot_split(y, s) for y, s in zip(ysp, ssp)]
-        zs = [dot_split(s, z) for s, z in zip(ssp, zsp)]
-    return zs
-
-
-def mix(root, rows_of, out, nu):
-    for u in range(nu):
+def inverse_root(e):
+    s0 = 1.5 * eye(2 * NB) - 0.5 * e
+    ep, s0p = split(e), split(s0)
+    m1 = dot_split(split(dot_split(ep, s0p)), s0p)
+    s1 = 1.5 * eye(2 * NB) - 0.5 * m1
+    m1p, s1p = split(m1), split(s1)
+    m1s = split(dot_split(m1p, s1p))
+    z2 = dot_split(s0p, s1p)
+    z2p = split(z2)
+    s1s = split(dot_split(s1p, s1p))
+    m2 = dot_split(m1s, s1p)
+    m2p = split(m2)
+    m1s2 = split(dot_split(m1s, m1s))
+    z2s2 = split(dot_split(z2p, s1s))
+    z2m = dot_split(z2p, m2p)
+    z2mm = dot_split(z2s2, m1s2)
+    mm = dot_split(m2p, m2p)
+    high = dot_split(split(z2mm), split(0.0625 * mm - 0.5625 * m2))
+    return (2.25 * z2 - 2.4375 * z2m + 1.6875 * z2mm) + high
+
+
+def mix(root, rows_of, out, units):
+    for u in units:
         y = dot(root, rows_of(u)).astype(BF16)
         cols = pl.ds(u // 3 * UNIT, UNIT)
         for i in range(2):
@@ -118,10 +119,14 @@
     for c in copies:
         c.start()
     y = normalized(cross_in[lf - 1, 0], cross_in[lf - 1, 1])
-    (root,) = inverse_roots([y])
-    mix(root.astype(BF16), lambda u: x[:, u * UNIT:(u + 1) * UNIT], out, nu)
-    copies.append(pltpu.make_async_copy(out, modes_ref.at[lf - 1], out_sem))
-    copies[-1].start()
+    root = inverse_root(y).astype(BF16)
+    for h in range(2):
+        mix(root, lambda u: x[:, u * UNIT:(u + 1) * UNIT], out,
+            range(h * nu // 2, (h + 1) * nu // 2))
+        at = (slice(None), slice(None), slice(None), pl.ds(h * nu // 6 * UNIT, nu // 6 * UNIT))
+        copies.append(pltpu.make_async_copy(
+            out.at[at], modes_ref.at[(lf - 1, *at)], out_sem.at[h]))
+        copies[-1].start()
     for c in copies:
         c.wait()
 
@@ -322,10 +327,10 @@
         return real, imag
 
     def finish(bins):
-        roots = inverse_roots([normalized(*collect(f)) for f in bins])
+        roots = [inverse_root(normalized(*collect(f))) for f in bins]
         for f, root in zip(bins, roots):
             mix(root.astype(BF16), lambda u: xall[f, :, u * UNIT:(u + 1) * UNIT],
-                early_ref.at[f], nu)
+                early_ref.at[f], range(nu))
 
     def arrived(p):
         stage(p - n_early + 1).wait_recv()
@@ -419,7 +424,7 @@
         scratch_shapes=[
             pltpu.VMEM((2, 3, NB, points), BF16),
             pltpu.SemaphoreType.DMA,
-            pltpu.SemaphoreType.DMA,
+            pltpu.SemaphoreType.DMA((2,)),
             pltpu.SemaphoreType.DMA,
         ],
         compiler_params=pltpu.CompilerParams(vmem_limit_bytes=16 * 2**20),

time: 34 us -> 33.8 us (level)
  no operation moved by 1% of the time
where the time goes in v5:
time: 33.8 us; the launch traced here: 33.7 us
  Pallas kernels  33 us (98%)
  between operations  0.64 us (2%)
    pallas_call x1, Pallas kernels, on_device(): pl.pallas_call(functools.partial(kernel, nt, ns, lf), out_shape=(jax.Shap...  31 us
    pallas_call x1, Pallas kernels, on_device(): pl.pallas_call(functools.partial(finish_kernel, nu), out_shape=(jax.Shape...  2.01 us

profile of v5, /device:TPU:0, one launch (start us, length us, event | category | flops | bytes accessed | tf_op | source)
XLA Modules:
  0.0 33.7 jit_solution(6676997820299704816)
XLA Ops:
  0.6 31.0 %shard_map.50 = (f32[4,2,32,32]{3,2,1,0:T(8,128)S(1)}, bf16[3,2,3,32,1024]{4,3,2,1,0:T(8,128)(2,1)S(1)}, bf16[64,3072]{1,0:T(8,128)(2,1)S(1)}) custom-call(bf16[3,2048,1024]{2,1,0:T(8,128)(2,1)} %bitcast.3, s32[16]{0:T(128)} %freq.1, f32[1,1024]{1,0:T(1,128)} %bitcast.4), custom_call_target="tpu_custom_call" | custom-call | tf_op jit(solution)/shard_map/pallas_call | solution.py:381
  31.7 2.0 %shard_map.51 = (f32[4,2,32,32]{3,2,1,0:T(8,128)}, bf16[4,2,3,32,1024]{4,3,2,1,0:T(8,128)(2,1)}) custom-call(f32[4,2,32,32]{3,2,1,0:T(8,128)S(1)} %get-tuple-element.7.cross_in, bf16[3,2,3,32,1024]{4,3,2,1,0:T(8,128)(2,1)S(1)} %get-tuple-element.8.early, bf16[64,3072]{1,0:T(8,128)(2,1)S(1)} %get-tuple-element.9.x), custom_call_target="tpu_custom_call" | custom-call | tf_op jit(solution)/shard_map/pallas_call | solution.py:416
